TPU v7x, 256 devices: a whole 4x4x8 slice. The times are simulated.
256 devices in a mesh: pipe: 8 (over z_hi, core), expert: 8 (over x, z_lo), tensor: 4 (over y).
Axes of the slice: x: 4, y: 4, z: 8 (z_hi: 4, z_lo: 2; z = z_hi * 2 + z_lo), core: 2. Of those that a mesh axis runs over, the one named last changes fastest.
Arguments:
- stream: bfloat16 [8, 2, 512, 4096], P('pipe', None, 'expert', 'tensor'), may hold values from -6 to 6
- expert_ids: int32 [8, 2, 512, 2], P('pipe', None, 'expert'), may hold values from 0 to 7, all different within a row; in each aligned block of 64 rows (0 to 63, 64 to 127, ..., all dimensions but the last counted through in order) at most 32 rows name the same one
- expert_gates: float32 [8, 2, 512, 2], P('pipe', None, 'expert'), may hold values from 0.1 to 1
- moe_gain: bfloat16 [8, 4096], P('pipe', 'tensor'), may hold values from 0.5 to 1.5
- w_gate: bfloat16 [8, 8, 4096, 1536], P('pipe', 'expert', None, 'tensor'), may hold values from -0.09375 to 0.09375
- w_up: bfloat16 [8, 8, 4096, 1536], P('pipe', 'expert', None, 'tensor'), may hold values from -0.09375 to 0.09375
- w_down: bfloat16 [8, 8, 1536, 4096], P('pipe', 'expert', 'tensor'), may hold values from -0.15625 to 0.15625
- attn_gain: bfloat16 [8, 4096], P('pipe', 'tensor'), may hold values from 0.5 to 1.5
- w_query: bfloat16 [8, 4096, 512], P('pipe', None, 'tensor'), may hold values from -3 to 3
- w_keyval: bfloat16 [8, 4096, 2, 512], P('pipe', None, None, 'tensor'), may hold values from -3 to 3
Outputs:
- moe_out: bfloat16 [8, 2, 512, 4096], P('pipe', None, 'expert', 'tensor')
- context: bfloat16 [8, 2, 512, 512], P('pipe', None, 'expert', 'tensor')
Inputs may be any that keep to these rules, and one draw needn't show every extreme that they name: `expert_ids`: in each aligned block of 64 positions of one sequence (the positions of one device), at most 32 positions name one expert; the two experts of a position differ.
All inputs are finite; a program needn't handle non-finite values.
Results may differ from a plain program's by a relative error of at most 0.02.
The roundings to bfloat16 on the way count: a program that leaves them out, or rounds other values in their place, can miss the bound.
Values may be sent and summed in bfloat16 or wider, within the bound.
A program may use at most 64 MiB of HBM per device.

v0:
```python
import jax
import jax.numpy as jnp
from jax import lax
from jax.sharding import PartitionSpec as P

HS = 128


EPS = 1e-05
THETA = 1000000.0
NEGATIVE = -1e30


def shifted(x, axis, by):
    size = lax.axis_size(axis)
    return lax.ppermute(x, axis, [(i, (i + by) % size) for i in range(size)])


def rms_scale(values, gain):
    floats = values.astype(jnp.float32)
    meansq = jnp.mean(floats * floats, axis=-1, keepdims=True)
    return (floats * lax.rsqrt(meansq + EPS) * gain.astype(jnp.float32)).astype(jnp.bfloat16)


def rotate(values, positions):
    heads = values.shape[-1] // HS
    shaped = values.reshape(values.shape[:-1] + (heads, HS))
    half_size = HS // 2
    freqs = jnp.exp(-jnp.log(THETA) * jnp.arange(half_size, dtype=jnp.float32) * 2.0 / HS)
    angles = positions[:, None] * freqs[None, :]
    cosine = jnp.cos(angles)[:, None, :]
    sine = jnp.sin(angles)[:, None, :]
    first = shaped[..., :half_size]
    second = shaped[..., half_size:]
    turned = jnp.concatenate(
        [first * cosine - second * sine, second * cosine + first * sine], axis=-1
    )
    return turned.reshape(values.shape)


def per_device(
    stream, expert_ids, expert_gates, moe_gain, w_gate, w_up, w_down, attn_gain, w_query, w_keyval
):
    local_rows = stream[0]
    micro, seq_dev, part_width = local_rows.shape
    full_width = part_width * lax.axis_size("tensor")
    experts = lax.axis_size("expert")
    capacity = min(seq_dev, 4 * seq_dev // experts)
    choices_count = seq_dev * 2
    local_ids = expert_ids[0].reshape(micro, choices_count)
    onehot = (local_ids[..., None] == jnp.arange(experts, dtype=jnp.int32)).astype(jnp.int32)
    ranks = jnp.cumsum(onehot, axis=1) - onehot
    slots = jnp.sum(ranks * onehot, axis=-1)
    targets = local_ids * capacity + slots
    placing = (
        targets[:, None, :] == jnp.arange(experts * capacity, dtype=jnp.int32)[None, :, None]
    ).astype(jnp.bfloat16)
    gate_weight = w_gate[0, 0]
    up_weight = w_up[0, 0]
    down_weight = w_down[0, 0]
    floats = local_rows.astype(jnp.float32)
    slot_count = micro * experts * capacity
    gathered, gain_full = (
        lax.all_gather(local_rows, "tensor", axis=2, tiled=True),
        lax.all_gather(moe_gain.reshape(1, 1, part_width), "tensor", axis=2, tiled=True),
    )
    normed = rms_scale(gathered, gain_full)
    doubled = jnp.repeat(normed, 2, axis=1)
    outgoing = jnp.einsum(
        "mja,mad->mjd", placing, doubled, preferred_element_type=jnp.float32
    ).astype(jnp.bfloat16)
    outgoing = outgoing.reshape(micro, experts, capacity, full_width)
    arrived = lax.all_to_all(outgoing, "expert", split_axis=1, concat_axis=1, tiled=True)
    inputs = arrived.reshape(slot_count, full_width)
    gated = jnp.dot(inputs, gate_weight, preferred_element_type=jnp.float32)
    lifted = jnp.dot(inputs, up_weight, preferred_element_type=jnp.float32)
    hidden = (jax.nn.silu(gated) * lifted).astype(jnp.bfloat16)
    partial_value = jnp.dot(hidden, down_weight, preferred_element_type=jnp.float32).reshape(
        micro, experts, capacity, full_width
    )
    summed = lax.psum_scatter(partial_value, "tensor", scatter_dimension=3, tiled=True).astype(
        jnp.bfloat16
    )
    returned = lax.all_to_all(summed, "expert", split_axis=1, concat_axis=1, tiled=True)
    picked = jnp.einsum(
        "mja,mjd->mad",
        placing,
        returned.reshape(micro, experts * capacity, part_width),
        preferred_element_type=jnp.float32,
    )
    weighted = picked * expert_gates[0].reshape(micro, choices_count)[..., None]
    combined = jnp.sum(weighted.reshape(micro, seq_dev, 2, part_width), axis=2)
    mixed = (floats + combined).astype(jnp.bfloat16)
    received = shifted(mixed, "pipe", 1)
    arrived_rows, attn_full = (
        lax.all_gather(received, "tensor", axis=2, tiled=True),
        lax.all_gather(attn_gain.reshape(1, 1, part_width), "tensor", axis=2, tiled=True),
    )
    anormed = rms_scale(arrived_rows, attn_full)
    flat = anormed.reshape(-1, full_width)
    query_positions = lax.axis_index("expert") * seq_dev + jnp.arange(seq_dev, dtype=jnp.int32)
    float_positions = query_positions.astype(jnp.float32)
    query = jnp.dot(flat, w_query[0], preferred_element_type=jnp.float32).reshape(
        micro, seq_dev, -1
    )
    query = rotate(query, float_positions).astype(jnp.bfloat16)
    key_width = w_keyval.shape[3]
    keyval = jnp.dot(
        flat, w_keyval[0].reshape(full_width, 2 * key_width), preferred_element_type=jnp.float32
    )
    keyval = keyval.reshape(micro, seq_dev, 2, key_width)
    keys = rotate(keyval[:, :, 0], float_positions).astype(jnp.bfloat16)
    values = keyval[:, :, 1].astype(jnp.bfloat16)
    kv_pair = jnp.stack([keys, values], axis=2)
    kv_heads = key_width // HS
    group_size = query.shape[2] // key_width
    query_heads = query.reshape(micro, seq_dev, kv_heads, group_size, HS)
    scale = HS ** (-0.5)
    start_max = jnp.full((micro, kv_heads, group_size, seq_dev), NEGATIVE, jnp.float32)
    piece = lax.all_gather(kv_pair, "expert", axis=1, tiled=True)
    length = piece.shape[1]
    key_piece = piece[:, :, 0].reshape(micro, length, kv_heads, HS)
    value_piece = piece[:, :, 1].reshape(micro, length, kv_heads, HS)
    scores = (
        jnp.einsum("mqkgd,mnkd->mkgqn", query_heads, key_piece, preferred_element_type=jnp.float32)
        * scale
    )
    key_positions = jnp.arange(length, dtype=jnp.int32)
    causal = key_positions[None, :] <= query_positions[:, None]
    scores = jnp.where(causal, scores, NEGATIVE)
    new_max = jnp.maximum(start_max, jnp.max(scores, axis=-1))
    weights = jnp.where(causal, jnp.exp(scores - new_max[..., None]), 0.0)
    new_total = jnp.sum(weights, axis=-1)
    added = jnp.einsum(
        "mkgqn,mnkd->mkgqd",
        weights.astype(jnp.bfloat16),
        value_piece,
        preferred_element_type=jnp.float32,
    )
    context = added / new_total[..., None]
    context = (
        jnp.transpose(context, (0, 3, 1, 2, 4)).reshape(micro, seq_dev, -1).astype(jnp.bfloat16)
    )
    return (mixed[None], context[None])


def solution(mesh):
    placed = (
        P("pipe", None, "expert", "tensor"),
        P("pipe", None, "expert", None),
        P("pipe", None, "expert", None),
        P("pipe", "tensor"),
        P("pipe", "expert", None, "tensor"),
        P("pipe", "expert", None, "tensor"),
        P("pipe", "expert", "tensor", None),
        P("pipe", "tensor"),
        P("pipe", None, "tensor"),
        P("pipe", None, None, "tensor"),
    )
    return jax.shard_map(
        per_device,
        mesh=mesh,
        in_specs=placed,
        out_specs=(P("pipe", None, "expert", "tensor"), P("pipe", None, "expert", "tensor")),
        check_vma=False,
    )
```

profile of v0, /device:TPU:32, one launch (start us, length us, event | category | flops | bytes accessed | tf_op | source)
XLA Modules:
  0.0 310.4 jit_solution(3127529931915629540)
XLA Ops:
  7.2 0.7 all-gather.8.cloned.1.call-update
  8.0 0.9 copy.25
  8.9 0.1 reshape_squeeze.6
  9.0 12.6 %all-gather.1 = bf16[1,4096]{1,0:T(2,128)(2,1)S(1)} all-gather(bf16[1,1024]{1,0:T(2,128)(2,1)} %param.13), channel_id=3, replica_groups=mesh['pipe'=8,'expert'=8,'tensor'=4] {'tensor'}, dimensions={1}, use_global_device_ids=true | all-gather | bytes 10240 | tf_op jit(solution)/shard_map/all_gather | solution.py:65
  21.7 0.1 fusion.38
  21.8 0.2 reduce_window_sum.11
  22.0 0.2 select_reduce_fusion
  22.1 16.9 %all-gather.8.cloned.1.call-done = bf16[1,2,64,4096]{3,2,1,0:T(8,128)(2,1)} async-done(((bf16[1,2,64,1024]{3,2,1,0:T(8,128)(2,1)}), bf16[1,2,64,4096]{3,2,1,0:T(8,128)(2,1)}) %all-gather.8.cloned.1.call-update) | async-done | bytes 1048592 | tf_op jit(solution)/shard_map/all_gather | solution.py:64
  39.0 1.5 fusion.9
  40.5 1.6 fusion.11
  42.1 3.4 %broadcast_in_dim.14 = bf16[2,64,2,4096]{3,2,1,0:T(2,128)(2,1)} broadcast(bf16[2,64,4096]{2,1,0:T(8,128)(2,1)S(1)} %fusion.11), dimensions={0,1,3} | broadcast | bytes 3145728 | tf_op jit(solution)/shard_map/broadcast_in_dim | solution.py:68
  45.6 4.1 %reshape.194 = bf16[2,128,4096]{2,1,0:T(8,128)(2,1)} reshape(bf16[2,64,2,4096]{3,2,1,0:T(2,128)(2,1)} %broadcast_in_dim.14) | data formatting | bytes 4194304 | tf_op jit(solution)/shard_map/reshape | solution.py:68
  49.7 2.9 convolution_convert_fusion
  52.6 0.5 copy.27
  53.1 52.9 %all_to_all.10 = bf16[2,8,32,4096]{3,2,0,1:T(8,128)(2,1)S(1)} all-to-all(bf16[2,8,32,4096]{3,2,0,1:T(8,128)(2,1)S(1)} %copy.27), channel_id=1, replica_groups=mesh['pipe'=8,'expert'=8,'tensor'=4] {'expert'}, dimensions={1} | all-to-all | bytes 8388608 | tf_op jit(solution)/shard_map/all_to_all | solution.py:73
  106.0 0.5 copy.28
  106.5 1.4 copy-done.5
  107.9 2.3 fusion.4
  110.2 2.4 fusion.15
  112.6 5.6 %fusion = f32[2,8,32,4096]{3,2,1,0:T(8,128)} fusion(bf16[2,8,32,384]{3,2,1,0:T(8,128)(2,1)S(1)} %bitcast.98, bf16[1,1,384,4096]{3,2,1,0:T(8,128)(2,1)S(1)} %copy-done), kind=kOutput, calls=%fused_computation.1 | convolution fusion | flops 1610612736 | bytes 11927552 | tf_op jit(solution)/shard_map/dot_general | solution.py:78
  118.2 81.5 %reduce-scatter.2.cloned.1.call-done = f32[2,8,32,1024]{3,2,1,0:T(8,128)} async-done(((f32[2,8,32,4096]{3,2,1,0:T(8,128)}), f32[2,8,32,1024]{3,2,1,0:T(8,128)}) %reduce-scatter.2.cloned.1.call-update) | async-done | bytes 2097168 | tf_op jit(solution)/shard_map/reduce_scatter | solution.py:81
  199.8 1.7 convert_element_type.78
  201.6 1.1 copy.29
  202.7 5.7 %all-to-all-start.1 = ((bf16[2,8,32,1024]{3,2,0,1:T(8,128)(2,1)}), bf16[2,8,32,1024]{3,2,0,1:T(8,128)(2,1)}, u32[]{:S(2)}, u32[]{:S(2)}) async-start(bf16[2,8,32,1024]{3,2,0,1:T(8,128)(2,1)} %copy.29), calls=%async_computation.2 | async-start | bytes 2097152 | tf_op jit(solution)/shard_map/all_to_all | solution.py:84
  208.4 0.1 copy.31
  208.5 0.1 mul.189
  208.7 14.4 %all-to-all-done.1 = bf16[2,8,32,1024]{3,2,0,1:T(8,128)(2,1)} async-done(((bf16[2,8,32,1024]{3,2,0,1:T(8,128)(2,1)}), bf16[2,8,32,1024]{3,2,0,1:T(8,128)(2,1)}, u32[]{:S(2)}, u32[]{:S(2)}) %all-to-all-start.1) | async-done | bytes 1048608 | tf_op jit(solution)/shard_map/all_to_all | solution.py:84
  223.1 1.3 copy.30
  224.4 1.4 convolution_multiply_fusion
  225.8 2.9 reshape.198
  228.7 3.3 %reduce_sum.49 = f32[2,64,1024]{2,1,0:T(8,128)} reduce(f32[2,64,2,1024]{3,2,1,0:T(2,128)} %reshape.198, f32[]{:T(128)} %constant.15.clone.1), dimensions={2}, to_apply=%region_4.5 | reduce | flops 131072 | bytes 1572868 | tf_op jit(solution)/shard_map/reduce_sum | solution.py:92
  232.0 1.1 fusion.29
  233.1 10.8 %collective-permute-done = bf16[2,64,1024]{2,1,0:T(8,128)(2,1)} collective-permute-done((bf16[2,64,1024]{2,1,0:T(8,128)(2,1)S(1)}, bf16[2,64,1024]{2,1,0:T(8,128)(2,1)}, u32[]{:S(2)}, u32[]{:S(2)}) %collective-permute-start) | collective-permute-done | bytes 262176 | tf_op jit(solution)/shard_map/ppermute | solution.py:16
  244.0 11.9 %all-gather.2 = bf16[1,4096]{1,0:T(2,128)(2,1)S(1)} all-gather(bf16[1,1024]{1,0:T(2,128)(2,1)S(1)} %copy-done.3), channel_id=4, replica_groups=mesh['pipe'=8,'expert'=8,'tensor'=4] {'tensor'}, dimensions={1}, use_global_device_ids=true | all-gather | bytes 10240 | tf_op jit(solution)/shard_map/all_gather | solution.py:97
  255.9 3.2 %copy.38 = bf16[512,8,2,128]{3,1,2,0:T(8,128)(2,1)} copy(bf16[512,8,2,128]{3,2,1,0:T(2,128)(2,1)} %bitcast.96) | data formatting | bytes 4194304
  259.1 4.1 %copy.32 = bf16[256,4096]{1,0:T(8,128)(2,1)} copy(bf16[256,4096]{0,1:T(8,128)(2,1)} %bitcast.92) | data formatting | bytes 4194304 | tf_op jit(solution)/shard_map/dot_general | solution.py:108
  263.3 0.1 iota_compare_fusion.3
  263.4 0.2 multiply_cosine_fusion
  263.6 1.8 fusion.27
  265.4 2.5 all-gather.6.cloned.1.call-done
  267.8 1.5 fusion.6
  269.4 2.9 fusion.22
  272.3 0.5 convolution_bitcast_fusion
  272.8 0.1 subtract_convert_fusion
  273.0 29.4 %all_gather.19 = bf16[2,512,2,128]{3,1,2,0:T(8,128)(2,1)S(1)} all-gather(bf16[2,64,2,128]{3,1,2,0:T(8,128)(2,1)S(1)} %pad_maximum_fusion), channel_id=1, replica_groups=mesh['pipe'=8,'expert'=8,'tensor'=4] {'expert'}, dimensions={1}, use_global_device_ids=true | all-gather | bytes 589824 | tf_op jit(solution)/shard_map/all_gather | solution.py:120
  302.4 0.3 fusion.45
  302.8 0.2 fusion.30
  303.0 0.9 fusion.21
  (32 shorter events, 0.4 us)
Async XLA Ops:
  7.2 105.5 %copy-start = (bf16[1,1,384,4096]{3,2,1,0:T(8,128)(2,1)S(1)}, bf16[1,1,384,4096]{3,2,1,0:T(8,128)(2,1)}, u32[]{:S(2)}) copy-start(bf16[1,1,384,4096]{3,2,1,0:T(8,128)(2,1)} %param.16) | copy-start | bytes 9437188
  7.2 31.8 %all-gather.8.cloned.1.call-start = ((), (), s32[]{:S(2)}) async-start(), calls=%async_computation.5 | async-start | bytes 1310720 | tf_op jit(solution)/shard_map/all_gather | solution.py:64
  7.9 191.9 %reduce-scatter.2.cloned.1.call-start = ((), (), s32[]{:S(2)}) async-start(), calls=%async_computation.3 | async-start | bytes 10485760 | tf_op jit(solution)/shard_map/reduce_scatter | solution.py:81
  106.0 1.9 copy-start.5
  107.9 2.3 copy-start.6
  201.5 6.9 %copy-start.4 = (f32[1,2,64,2]{2,3,1,0:T(2,128)S(1)}, f32[1,2,64,2]{2,3,1,0:T(2,128)}, u32[]{:S(2)}) copy-start(f32[1,2,64,2]{2,3,1,0:T(2,128)} %param.12) | copy-start | bytes 3076
  202.7 20.4 %all-to-all-start.1 = ((bf16[2,8,32,1024]{3,2,0,1:T(8,128)(2,1)}), bf16[2,8,32,1024]{3,2,0,1:T(8,128)(2,1)}, u32[]{:S(2)}, u32[]{:S(2)}) async-start(bf16[2,8,32,1024]{3,2,0,1:T(8,128)(2,1)} %copy.29), calls=%async_computation.2 | async-start | bytes 2097152 | tf_op jit(solution)/shard_map/all_to_all | solution.py:84
  208.4 59.5 %all-gather.6.cloned.1.call-start = ((), (), s32[]{:S(2)}) async-start(), calls=%async_computation.4 | async-start | bytes 1310720 | tf_op jit(solution)/shard_map/all_gather | solution.py:96
  225.8 6.2 %copy-start.1 = (bf16[1,2,64,1024]{3,2,1,0:T(8,128)(2,1)S(1)}, bf16[1,2,64,1024]{3,2,1,0:T(8,128)(2,1)}, u32[]{:S(2)}) copy-start(bf16[1,2,64,1024]{3,2,1,0:T(8,128)(2,1)} %param.10) | copy-start | bytes 786436
  225.8 18.2 %copy-start.3 = (bf16[1,1024]{1,0:T(2,128)(2,1)S(1)}, bf16[1,1024]{1,0:T(2,128)(2,1)}, u32[]{:S(2)}) copy-start(bf16[1,1024]{1,0:T(2,128)(2,1)} %param.17) | copy-start | bytes 6148
  233.1 10.9 %collective-permute-start = (bf16[2,64,1024]{2,1,0:T(8,128)(2,1)S(1)}, bf16[2,64,1024]{2,1,0:T(8,128)(2,1)}, u32[]{:S(2)}, u32[]{:S(2)}) collective-permute-start(bf16[2,64,1024]{2,1,0:T(8,128)(2,1)S(1)} %fusion.29), channel_id=1, source_target_pairs={{0,32},{32,64},{64,96},{96,128},{128,160},{160,192},{192,224},{224... | collective-permute-start | bytes 786440 | tf_op jit(solution)/shard_map/ppermute | solution.py:16
  269.4 2.9 copy-start.2
  269.4 2.9 copy-start.7
Sparse Core Ops, SparseCore 0:
  9.8 29.1 all-gather.7
  118.4 81.3 reduce-scatter.1
  244.1 23.6 all-gather.5
where the time goes:
time: 312 us; the launch traced here: 310 us
  waiting for transfers between devices  127 us (41%)
  blocking collectives  107 us (34%)
  local copies, waits for them, and re-layouts  23.9 us (8%)
  matrix products  19.2 us (6%)
  between operations  14 us (4%)
  other arithmetic  13.8 us (4%)
  starting transfers between devices  5.87 us (2%)
    reduce_scatter x1, waiting for transfers between devices, per_device(): lax.psum_scatter(partial_value, 'tensor', scatter_dimension=3, tiled=True)  81.5 us
    all_to_all x1, blocking collectives, per_device(): lax.all_to_all(outgoing, 'expert', split_axis=1, concat_axis=1, tiled=True)  52.9 us
    all_gather x1, blocking collectives, per_device(): piece = lax.all_gather(kv_pair, 'expert', axis=1, tiled=True)  29.4 us
    all_gather x1, waiting for transfers between devices, per_device(): lax.all_gather(local_rows, 'tensor', axis=2, tiled=True)  16.9 us
    all_to_all x1, waiting for transfers between devices, per_device(): lax.all_to_all(summed, 'expert', split_axis=1, concat_axis=1, tiled=True)  14.4 us
    all_gather x1, blocking collectives, per_device(): lax.all_gather(moe_gain.reshape(1, 1, part_width), 'tensor', axis=2, tile...  12.6 us
    all_gather x1, blocking collectives, per_device(): lax.all_gather(attn_gain.reshape(1, 1, part_width), 'tensor', axis=2, til...  11.9 us
    ppermute x1, waiting for transfers between devices, shifted(): return lax.ppermute(x, axis, [(i, (i + by) % size) for i in range(size)])  10.8 us
  transfers between devices with their start and end apart: 5, of which 5 were waited for; matrix products, arithmetic and copies ran while one was open for 4% of the time, Pallas kernels for 0%

commit v1 on v0

v1 whole, which is shorter than its diff:
```python
import jax
import jax.numpy as jnp
import numpy as np
from jax import lax
from jax.experimental import pallas as pl
from jax.experimental.pallas import tpu as pltpu
from jax.sharding import PartitionSpec as P

MESH = pl.DeviceIdType.MESH
HS = 128
EPS = 1e-05
THETA = 1000000.0
NEGATIVE = -1e30
F32 = jnp.float32
BF16 = jnp.bfloat16
I16 = jnp.int16

MICRO = 2
ROWS = 64
PART = 1024
CAP = 32
EXPERTS = 8
SLOTS = EXPERTS * CAP
HALF = SLOTS // 2
CUTS = 2
WIDE = PART // CUTS
FF = 384
LENGTH = EXPERTS * ROWS
RIGHT, OPPOSITE, LEFT = 1, 2, 3
SEMAPHORES = 160


def rope_table(length):
    freqs = THETA ** (-2.0 * np.arange(HS // 2) / HS)
    angles = np.arange(length)[:, None] * freqs[None, :]
    cosine, sine = np.cos(angles), np.sin(angles)
    return np.concatenate([cosine, cosine, -sine, sine], axis=1).astype(np.float32)


class Group:
    def __init__(self, sem, whole):
        self.sem, self.whole, self.sent, self.waited = sem, whole, False, False


class Messages:
    def __init__(self, sems):
        self.sems, self.used, self.sends, self.recvs = sems, 0, [], []

    def group(self, whole, kind):
        found = Group(self.sems.at[self.used], whole)
        self.used += 1
        kind.append(found)
        return found

    def leaving(self, whole):
        return self.group(whole, self.sends)

    def coming(self, whole):
        return self.group(whole, self.recvs)

    def send(self, src, dst, leaving, coming, **where):
        pltpu.make_async_remote_copy(
            src_ref=src,
            dst_ref=dst,
            send_sem=leaving.sem,
            recv_sem=coming.sem,
            device_id=where,
            device_id_type=MESH,
        ).start()
        leaving.sent = coming.sent = True

    def _any(self, found):
        return pltpu.make_async_remote_copy(
            src_ref=found.whole,
            dst_ref=found.whole,
            send_sem=found.sem,
            recv_sem=found.sem,
            device_id={"tensor": lax.rem(lax.axis_index("tensor") + 1, 4)},
            device_id_type=MESH,
        )

    def wait(self, found):
        self._any(found).wait_recv()
        found.waited = True

    def finish(self):
        for found in self.recvs:
            if found.sent and not found.waited:
                self.wait(found)
        for found in self.sends:
            if found.sent:
                self._any(found).wait_send()


def dot(a, b):
    return jnp.dot(a, b, preferred_element_type=F32)


def dot_first(a, b):
    return lax.dot_general(a, b, (((0,), (0,)), ((), ())), preferred_element_type=F32)


def flipped(line):
    n = max(line.shape)
    diagonal = lax.broadcasted_iota(jnp.int32, (n, n), 0) == lax.broadcasted_iota(
        jnp.int32, (n, n), 1
    )
    axis = 0 if line.shape[1] == 1 else 1
    return jnp.sum(jnp.where(diagonal, line, 0.0), axis=axis, keepdims=True)


def encoded(value):
    highest = jnp.maximum(jnp.max(jnp.abs(value), axis=1, keepdims=True), 1e-30)
    codes = jnp.round(value * (32760.0 / highest)).astype(jnp.int32).astype(I16)
    return codes, highest * (1.0 / 32760.0)


def decoded(codes, step):
    return codes.astype(jnp.int32).astype(F32) * step


def kernel(
    stream_hbm, ids_hbm, gates_hbm, mgain_hbm, again_hbm,
    wg_hbm, wu_hbm, wd_hbm, wq_hbm, wkv_hbm, rope_hbm,
    moe_out, context_out,
    stream, ids, gates, mgain, again, w13, wd, wqkv, wkv, rope,
    ssq, gains, out, x, acc, hidden,
    opp, going_r, going_l, part_r, part_l, own, opp_l, opp_r, sum_l, sum_r,
    steps_r, steps_l, steps_from_r, steps_from_l, more_r, more_l, more_from_r, more_from_l,
    eo, ret, mixed, rows_in, kv_own, kv_in, context,
    local_sems, sems,
):
    e, t, p = lax.axis_index("expert"), lax.axis_index("tensor"), lax.axis_index("pipe")
    right, left, opposite = lax.rem(t + 1, 4), lax.rem(t + 3, 4), lax.rem(t + 2, 4)
    after, before = lax.rem(p + 1, 8), lax.rem(p + 7, 8)
    peer = [lax.rem(e + o, EXPERTS) for o in range(EXPERTS)]
    msg = Messages(sems)

    here = pl.ds(pl.multiple_of(e * ROWS, ROWS), ROWS)
    loads = [
        (stream_hbm, stream),
        (ids_hbm, ids),
        (mgain_hbm, mgain),
        (gates_hbm, gates),
        (again_hbm, again),
        (wg_hbm, w13.at[:, :FF]),
        (wu_hbm, w13.at[:, FF:]),
        (wd_hbm, wd),
        (wq_hbm, wqkv.at[:, :HS]),
        (wkv_hbm, wkv),
        (rope_hbm.at[here], rope),
    ]
    loads = [pltpu.make_async_copy(s, d, local_sems.at[i]) for i, (s, d) in enumerate(loads)]
    for load in loads:
        load.start()

    barrier = pltpu.get_barrier_semaphore()
    peers = [{"expert": other} for other in peer[1:]]
    peers += [{"tensor": other} for other in (right, left, opposite)]
    peers += [{"pipe": other} for other in (after, before)]
    for other in peers:
        pl.semaphore_signal(barrier, inc=1, device_id=other, device_id_type=MESH)

    slot = lax.broadcasted_iota(jnp.int32, (SLOTS, ROWS), 0)
    group, place = slot // CAP, slot % CAP
    expert_of = jnp.where(group + e >= EXPERTS, group + e - EXPERTS, group + e)
    row_of = lax.broadcasted_iota(jnp.int32, (ROWS, ROWS), 0)
    col_of = lax.broadcasted_iota(jnp.int32, (ROWS, ROWS), 1)
    earlier = jnp.where(row_of < col_of, 1.0, 0.0).astype(BF16)
    for load in loads[:5]:
        load.wait()
    chosen = []
    for m in range(MICRO):
        first = ids[m, 0:1, :] == expert_of
        second = ids[m, 1:2, :] == expert_of
        named = jnp.where(first | second, 1.0, 0.0)
        taken = dot(named.astype(BF16), earlier) == place.astype(F32)
        chosen.append(
            [jnp.where(which & taken, 1.0, 0.0).astype(BF16) for which in (first, second)]
        )

    value = stream[...].reshape(MICRO * ROWS, PART).astype(F32)
    ssq[0] = jnp.broadcast_to(flipped(jnp.sum(value * value, axis=1, keepdims=True)), (8, MICRO * ROWS))
    gains[0] = jnp.broadcast_to(again[...], (16, PART))

    pl.semaphore_wait(barrier, len(peers))

    def to_tensor_peers(buffer):
        leaving, coming = msg.leaving(buffer.at[1:4]), msg.coming(buffer.at[1:4])
        for rel, other in ((RIGHT, right), (LEFT, left), (OPPOSITE, opposite)):
            msg.send(buffer.at[0], buffer.at[rel], leaving, coming, tensor=other)
        return coming

    msg.wait(to_tensor_peers(ssq))
    total = (ssq[0, 0:1, :] + ssq[1, 0:1, :]) + (ssq[2, 0:1, :] + ssq[3, 0:1, :])
    scales = flipped(lax.rsqrt(total * (1.0 / (4 * PART)) + EPS))

    out_leave = [msg.leaving(out.at[m, 1:]) for m in range(MICRO)]
    out_come = [[None] + [msg.coming(x.at[m, 0, o]) for o in range(1, EXPERTS)] for m in range(MICRO)]
    x_leave_r = [msg.leaving(x.at[m, 0]) for m in range(MICRO)]
    x_leave_l = [msg.leaving(x.at[m, 0]) for m in range(MICRO)]
    near = EXPERTS // 2
    x_come_r = [
        [msg.coming(x.at[m, RIGHT, o]) for o in range(near)] + [msg.coming(x.at[m, RIGHT, near:])] * near
        for m in range(MICRO)
    ]
    x_come_l = [
        [msg.coming(x.at[m, LEFT, :near])] * near + [msg.coming(x.at[m, LEFT, o]) for o in range(near, EXPERTS)]
        for m in range(MICRO)
    ]
    ahead_leave_r = [msg.leaving(x.at[m, RIGHT, :near]) for m in range(MICRO)]
    ahead_leave_l = [msg.leaving(x.at[m, LEFT, near:]) for m in range(MICRO)]
    ahead_come_r = [msg.coming(x.at[m, OPPOSITE, :near]) for m in range(MICRO)]
    ahead_come_l = [msg.coming(x.at[m, OPPOSITE, near:]) for m in range(MICRO)]

    def place_rows(m):
        scale = scales[m * ROWS : (m + 1) * ROWS]
        normed = (stream[m].astype(F32) * scale * mgain[...].astype(F32)).astype(BF16)
        block = dot(chosen[m][0] + chosen[m][1], normed).astype(BF16).reshape(EXPERTS, CAP, PART)
        x[m, 0, 0] = block[0]
        out[m] = block

    def dispatch(m):
        for o in range(1, EXPERTS):
            msg.send(out.at[m, o], x.at[m, 0, o], out_leave[m], out_come[m][o], expert=peer[o])

    def gather_send(m, pieces):
        for o in pieces:
            if o > 0:
                msg.wait(out_come[m][o])
            msg.send(x.at[m, 0, o], x.at[m, RIGHT, o], x_leave_r[m], x_come_r[m][o], tensor=right)
            msg.send(x.at[m, 0, o], x.at[m, LEFT, o], x_leave_l[m], x_come_l[m][o], tensor=left)

    def gather_forward(m):
        for i in range(near):
            msg.wait(x_come_r[m][i])
            msg.send(x.at[m, RIGHT, i], x.at[m, OPPOSITE, i], ahead_leave_r[m], ahead_come_r[m], tensor=right)
            o = i + near
            msg.wait(x_come_l[m][o])
            msg.send(x.at[m, LEFT, o], x.at[m, OPPOSITE, o], ahead_leave_l[m], ahead_come_l[m], tensor=left)

    def quarter(rel):
        return pl.ds(pl.multiple_of(lax.rem(t + 4 - rel, 4) * PART, PART), PART)

    def expert_in(m, rel):
        value = dot(x[m, rel].reshape(SLOTS, PART), w13[quarter(rel), :])
        acc[...] = value if rel == 0 else acc[...] + value

    def activate(m):
        gated, lifted = acc[:, :FF], acc[:, FF:]
        hidden[m] = (gated / (1.0 + jnp.exp(-gated)) * lifted).astype(BF16)

    def pairs(buffer, kind):
        return [kind(buffer.at[m]) for m in range(MICRO)]

    def each(buffer, rows):
        return [[msg.coming(buffer.at[m, c, rows]) for c in range(CUTS)] for m in range(MICRO)]

    top, low, every = slice(0, HALF), slice(HALF, SLOTS), slice(None)
    opp_leave, going_r_leave, going_l_leave = (
        pairs(b, msg.leaving) for b in (opp, going_r, going_l)
    )
    steps_r_leave, steps_l_leave, more_r_leave, more_l_leave = (
        pairs(b, msg.leaving) for b in (steps_r, steps_l, more_r, more_l)
    )
    opp_l_come, opp_r_come = each(opp_l, every), each(opp_r, every)
    sum_l_top, sum_l_low = each(sum_l, top), each(sum_l, low)
    sum_r_top, sum_r_low = each(sum_r, top), each(sum_r, low)
    steps_l_come, steps_r_come = each(steps_from_l, every), each(steps_from_r, every)
    more_l_come, more_r_come = each(more_from_l, every), each(more_from_r, every)

    def part(m, c, rel):
        at = pl.multiple_of(lax.rem(t + rel, 4) * PART + c * WIDE, WIDE)
        return dot(hidden[m], wd[:, pl.ds(at, WIDE)])

    def send_opposite(m, c):
        opp[m, c], step = encoded(part(m, c, OPPOSITE))
        for ref in (steps_r, steps_l, more_r, more_l):
            ref[m, c] = jnp.zeros((8, HALF), F32)
        steps_r[m, c, 0:1] = flipped(step[:HALF])
        steps_l[m, c, 0:1] = flipped(step[HALF:])
        msg.send(opp.at[m, c, top], opp_l.at[m, c], opp_leave[m], opp_l_come[m][c], tensor=right)
        msg.send(opp.at[m, c, low], opp_r.at[m, c], opp_leave[m], opp_r_come[m][c], tensor=left)

    def send_direct(m, c):
        value = part(m, c, RIGHT)
        part_r[m, c] = value[:HALF]
        going_r[m, c, low], step = encoded(value[HALF:])
        steps_r[m, c, 1:2] = flipped(step)
        msg.send(steps_r.at[m, c], steps_from_l.at[m, c], steps_r_leave[m], steps_l_come[m][c], tensor=right)
        msg.send(going_r.at[m, c, low], sum_l.at[m, c, low], going_r_leave[m], sum_l_low[m][c], tensor=right)
        value = part(m, c, LEFT)
        part_l[m, c] = value[HALF:]
        going_l[m, c, top], step = encoded(value[:HALF])
        steps_l[m, c, 1:2] = flipped(step)
        msg.send(steps_l.at[m, c], steps_from_r.at[m, c], steps_l_leave[m], steps_r_come[m][c], tensor=left)
        msg.send(going_l.at[m, c, top], sum_r.at[m, c, top], going_l_leave[m], sum_r_top[m][c], tensor=left)

    def sum_middle(m, c):
        msg.wait(steps_l_come[m][c])
        msg.wait(opp_l_come[m][c])
        value = part_r[m, c] + decoded(opp_l[m, c], flipped(steps_from_l[m, c, 0:1]))
        going_r[m, c, top], step = encoded(value)
        more_r[m, c, 0:1] = flipped(step)
        msg.send(more_r.at[m, c], more_from_l.at[m, c], more_r_leave[m], more_l_come[m][c], tensor=right)
        msg.send(going_r.at[m, c, top], sum_l.at[m, c, top], going_r_leave[m], sum_l_top[m][c], tensor=right)
        msg.wait(steps_r_come[m][c])
        msg.wait(opp_r_come[m][c])
        value = part_l[m, c] + decoded(opp_r[m, c], flipped(steps_from_r[m, c, 0:1]))
        going_l[m, c, low], step = encoded(value)
        more_l[m, c, 0:1] = flipped(step)
        msg.send(more_l.at[m, c], more_from_r.at[m, c], more_l_leave[m], more_r_come[m][c], tensor=left)
        msg.send(going_l.at[m, c, low], sum_r.at[m, c, low], going_l_leave[m], sum_r_low[m][c], tensor=left)

    eo_leave = [msg.leaving(eo.at[m, :, 1:]) for m in range(MICRO)]
    ret_come = [[msg.coming(ret.at[m, c, 1:]) for c in range(CUTS)] for m in range(MICRO)]

    def sum_last(m, c):
        for found in (sum_l_low, sum_r_top, more_l_come, sum_l_top, more_r_come, sum_r_low):
            msg.wait(found[m][c])
        above = own[m, c, top] + (
            decoded(sum_l[m, c, top], flipped(more_from_l[m, c, 0:1]))
            + decoded(sum_r[m, c, top], flipped(steps_from_r[m, c, 1:2]))
        )
        below = own[m, c, low] + (
            decoded(sum_l[m, c, low], flipped(steps_from_l[m, c, 1:2]))
            + decoded(sum_r[m, c, low], flipped(more_from_r[m, c, 0:1]))
        )
        value = jnp.concatenate([above.astype(BF16), below.astype(BF16)], axis=0)
        value = value.reshape(EXPERTS, CAP, WIDE)
        ret[m, c, 0] = value[0]
        eo[m, c] = value
        for o in range(1, EXPERTS):
            msg.send(
                eo.at[m, c, o], ret.at[m, c, o], eo_leave[m], ret_come[m][c],
                expert=lax.rem(e + EXPERTS - o, EXPERTS),
            )

    mixed_leave = [msg.leaving(mixed.at[m]) for m in range(MICRO)]
    moe_writes = []
    shift_come = [[msg.coming(rows_in.at[m, 0, c]) for c in range(CUTS)] for m in range(MICRO)]

    def combine(m, c):
        msg.wait(ret_come[m][c])
        returned = ret[m, c].reshape(SLOTS, WIDE)
        columns = slice(c * WIDE, (c + 1) * WIDE)
        value = None
        for k in range(2):
            term = flipped(gates[m, k : k + 1, :]) * dot_first(chosen[m][k], returned)
            value = term if value is None else value + term
        mixed[m, c] = (stream[m, :, columns].astype(F32) + value).astype(BF16)
        msg.send(mixed.at[m, c], rows_in.at[m, 0, c], mixed_leave[m], shift_come[m][c], pipe=after)
        number = len(loads) + len(moe_writes)
        moe_writes.append(
            pltpu.make_async_copy(mixed.at[m, c], moe_out.at[m, :, columns], local_sems.at[number])
        )
        moe_writes[-1].start()

    half = ROWS // 2
    rows_leave_r, rows_leave_l = (
        [msg.leaving(rows_in.at[m, 0]) for m in range(MICRO)] for _ in range(2)
    )
    rows_ahead_r = [msg.leaving(rows_in.at[m, RIGHT, :, :half]) for m in range(MICRO)]
    rows_ahead_l = [msg.leaving(rows_in.at[m, LEFT, :, half:]) for m in range(MICRO)]
    rows_come_r, rows_come_l = (
        [[msg.coming(rows_in.at[m, rel, c]) for c in range(CUTS)] for m in range(MICRO)]
        for rel in (RIGHT, LEFT)
    )
    rows_far_r = [[msg.coming(rows_in.at[m, OPPOSITE, c, :half]) for c in range(CUTS)] for m in range(MICRO)]
    rows_far_l = [[msg.coming(rows_in.at[m, OPPOSITE, c, half:]) for c in range(CUTS)] for m in range(MICRO)]

    def rows_send(m, c):
        msg.wait(shift_come[m][c])
        msg.send(rows_in.at[m, 0, c], rows_in.at[m, RIGHT, c], rows_leave_r[m], rows_come_r[m][c], tensor=right)
        msg.send(rows_in.at[m, 0, c], rows_in.at[m, LEFT, c], rows_leave_l[m], rows_come_l[m][c], tensor=left)

    def rows_forward(m, c):
        msg.wait(rows_come_r[m][c])
        msg.send(
            rows_in.at[m, RIGHT, c, :half], rows_in.at[m, OPPOSITE, c, :half],
            rows_ahead_r[m], rows_far_r[m][c], tensor=right,
        )
        msg.wait(rows_come_l[m][c])
        msg.send(
            rows_in.at[m, LEFT, c, half:], rows_in.at[m, OPPOSITE, c, half:],
            rows_ahead_l[m], rows_far_l[m][c], tensor=left,
        )

    kv_leave = [msg.leaving(kv_in.at[m, 1:]) for m in range(MICRO)]
    kv_come = [msg.coming(kv_in.at[m, 1:]) for m in range(MICRO)]

    def turned(value):
        swapped = pltpu.roll(value, HS // 2, 1)
        return (value * rope[:, :HS] + swapped * rope[:, HS:]).astype(BF16)

    def project(m):
        for c in range(CUTS):
            msg.wait(rows_far_r[m][c])
            msg.wait(rows_far_l[m][c])
        total = None
        for rel in range(4):
            for c in range(CUTS):
                value = rows_in[m, rel, c].astype(F32)
                term = jnp.sum(value * value, axis=-1, keepdims=True)
                total = term if total is None else total + term
        scale = lax.rsqrt(total * (1.0 / (4 * PART)) + EPS)
        result = None
        for rel in range(4):
            for c in range(CUTS):
                gain = gains[rel, 0:1, c * WIDE : (c + 1) * WIDE].astype(F32)
                normed = (rows_in[m, rel, c].astype(F32) * scale * gain).astype(BF16)
                at = pl.multiple_of(lax.rem(t + 4 - rel, 4) * PART + c * WIDE, WIDE)
                term = dot(normed, wqkv[pl.ds(at, WIDE), :])
                result = term if result is None else result + term
        query = turned(result[:, :HS])
        key = turned(result[:, HS : 2 * HS])
        kv = jnp.concatenate([key, result[:, 2 * HS :].astype(BF16)], axis=1)
        kv_own[m] = kv
        kv_in[m, 0] = kv
        for o in range(1, EXPERTS):
            msg.send(kv_own.at[m], kv_in.at[m, o], kv_leave[m], kv_come[m], expert=peer[o])
        return query

    def attend(m, query):
        column = lax.broadcasted_iota(jnp.int32, (ROWS, LENGTH), 1)
        source = e - column // ROWS
        source = jnp.where(source < 0, source + EXPERTS, source)
        row = e * ROWS + lax.broadcasted_iota(jnp.int32, (ROWS, LENGTH), 0)
        causal = source * ROWS + column % ROWS <= row
        msg.wait(kv_come[m])
        kv = kv_in[m].reshape(LENGTH, 2 * HS)
        scores = lax.dot_general(
            query, kv[:, :HS], (((1,), (1,)), ((), ())), preferred_element_type=F32
        )
        scores = jnp.where(causal, scores * HS ** (-0.5), NEGATIVE)
        highest = jnp.max(scores, axis=-1, keepdims=True)
        weights = jnp.where(causal, jnp.exp(scores - highest), 0.0)
        total = jnp.sum(weights, axis=-1, keepdims=True)
        context[m] = (dot(weights.astype(BF16), kv[:, HS:]) / total).astype(BF16)

    def split_weights():
        step = 512
        row = lax.broadcasted_iota(jnp.int32, (step // 2, step), 0)
        col = lax.broadcasted_iota(jnp.int32, (step // 2, step), 1)

        def body(i, _):
            block = wkv[pl.ds(pl.multiple_of(i * step, step), step), :]
            to = pl.ds(pl.multiple_of(i * (step // 2), step // 2), step // 2)
            for k in range(2):
                pick = jnp.where(col == 2 * row + k, 1.0, 0.0).astype(BF16)
                wqkv[to, (k + 1) * HS : (k + 2) * HS] = dot(pick, block).astype(BF16)
            return 0

        lax.fori_loop(0, wkv.shape[0] // step, body, 0)

    place_rows(0)
    dispatch(0)
    gather_send(0, [0])
    place_rows(1)
    gather_send(0, [1, 2, 3, 4])
    dispatch(1)
    gather_send(0, [5, 6, 7])
    gains_come = to_tensor_peers(gains)
    for load in loads[5:]:
        load.wait()
    expert_in(0, 0)
    gather_forward(0)
    gather_send(1, range(EXPERTS))
    split_weights()
    msg.wait(x_come_r[0][near])
    expert_in(0, RIGHT)
    msg.wait(x_come_l[0][0])
    expert_in(0, LEFT)
    msg.wait(ahead_come_r[0])
    msg.wait(ahead_come_l[0])
    expert_in(0, OPPOSITE)
    activate(0)
    for c in range(CUTS):
        send_opposite(0, c)
        send_direct(0, c)
    for c in range(CUTS):
        own[0, c] = part(0, c, 0)
    expert_in(1, 0)
    gather_forward(1)
    for c in range(CUTS):
        sum_middle(0, c)
    msg.wait(x_come_r[1][near])
    expert_in(1, RIGHT)
    msg.wait(x_come_l[1][0])
    expert_in(1, LEFT)
    msg.wait(ahead_come_r[1])
    msg.wait(ahead_come_l[1])
    expert_in(1, OPPOSITE)
    activate(1)
    send_opposite(1, 0)
    send_direct(1, 0)
    send_opposite(1, 1)
    sum_last(0, 0)
    sum_middle(1, 0)
    send_direct(1, 1)
    sum_last(0, 1)
    for c in range(CUTS):
        own[1, c] = part(1, c, 0)
    sum_middle(1, 1)
    combine(0, 0)
    combine(0, 1)
    sum_last(1, 0)
    rows_send(0, 0)
    rows_send(0, 1)
    sum_last(1, 1)
    msg.wait(gains_come)
    rows_forward(0, 0)
    rows_forward(0, 1)
    combine(1, 0)
    query0 = project(0)
    combine(1, 1)
    rows_send(1, 0)
    rows_send(1, 1)
    attend(0, query0)
    rows_forward(1, 0)
    rows_forward(1, 1)
    query1 = project(1)
    attend(1, query1)

    writes = [
        pltpu.make_async_copy(context, context_out, local_sems.at[len(loads) + len(moe_writes)])
    ]
    writes[0].start()
    for write in writes + moe_writes:
        write.wait()
    msg.finish()


def per_device(
    stream, expert_ids, expert_gates, moe_gain, w_gate, w_up, w_down, attn_gain, w_query, w_keyval
):
    hbm = pl.BlockSpec(memory_space=pl.ANY)
    slots_cut = (MICRO, CUTS, SLOTS, WIDE)
    half_cut = (MICRO, CUTS, HALF, WIDE)
    scratch = [
        ((MICRO, ROWS, PART), BF16),
        ((MICRO, 2, ROWS), jnp.int32),
        ((MICRO, 2, ROWS), F32),
        ((1, PART), BF16),
        ((1, PART), BF16),
        ((4 * PART, 2 * FF), BF16),
        ((FF, 4 * PART), BF16),
        ((4 * PART, 3 * HS), BF16),
        ((8 * PART, HS), BF16),
        ((ROWS, 2 * HS), F32),
        ((4, 8, MICRO * ROWS), F32),
        ((4, 16, PART), BF16),
        ((MICRO, EXPERTS, CAP, PART), BF16),
        ((MICRO, 4, EXPERTS, CAP, PART), BF16),
        ((SLOTS, 2 * FF), F32),
        ((MICRO, SLOTS, FF), BF16),
        (slots_cut, I16),
        (slots_cut, I16),
        (slots_cut, I16),
        (half_cut, F32),
        (half_cut, F32),
        (slots_cut, F32),
        (half_cut, I16),
        (half_cut, I16),
        (slots_cut, I16),
        (slots_cut, I16),
    ]
    scratch += [((MICRO, CUTS, 8, HALF), F32)] * 8
    scratch += [
        ((MICRO, CUTS, EXPERTS, CAP, WIDE), BF16),
        ((MICRO, CUTS, EXPERTS, CAP, WIDE), BF16),
        ((MICRO, CUTS, ROWS, WIDE), BF16),
        ((MICRO, 4, CUTS, ROWS, WIDE), BF16),
        ((MICRO, ROWS, 2 * HS), BF16),
        ((MICRO, EXPERTS, ROWS, 2 * HS), BF16),
        ((MICRO, ROWS, HS), BF16),
    ]
    moe, context = pl.pallas_call(
        kernel,
        out_shape=(
            jax.ShapeDtypeStruct((MICRO, ROWS, PART), BF16),
            jax.ShapeDtypeStruct((MICRO, ROWS, HS), BF16),
        ),
        in_specs=[hbm] * 11,
        out_specs=(hbm, hbm),
        scratch_shapes=[pltpu.VMEM(shape, kind) for shape, kind in scratch]
        + [pltpu.SemaphoreType.DMA((16,)), pltpu.SemaphoreType.DMA((SEMAPHORES,))],
        compiler_params=pltpu.CompilerParams(
            collective_id=0, has_side_effects=True, vmem_limit_bytes=56 * 1024 * 1024
        ),
        cost_estimate=pl.CostEstimate(
            flops=5_300_000_000, bytes_accessed=13_000_000, transcendentals=500_000
        ),
    )(
        stream[0],
        jnp.transpose(expert_ids[0], (0, 2, 1)),
        jnp.transpose(expert_gates[0], (0, 2, 1)),
        moe_gain,
        attn_gain,
        w_gate[0, 0],
        w_up[0, 0],
        w_down[0, 0],
        w_query[0],
        w_keyval[0].reshape(8 * PART, HS),
        jnp.asarray(rope_table(LENGTH)),
    )
    return moe[None], context[None]


def solution(mesh):
    placed = (
        P("pipe", None, "expert", "tensor"),
        P("pipe", None, "expert", None),
        P("pipe", None, "expert", None),
        P("pipe", "tensor"),
        P("pipe", "expert", None, "tensor"),
        P("pipe", "expert", None, "tensor"),
        P("pipe", "expert", "tensor", None),
        P("pipe", "tensor"),
        P("pipe", None, "tensor"),
        P("pipe", None, None, "tensor"),
    )
    return jax.shard_map(
        per_device,
        mesh=mesh,
        in_specs=placed,
        out_specs=(P("pipe", None, "expert", "tensor"), P("pipe", None, "expert", "tensor")),
        check_vma=False,
    )
```

time: 312 us -> 117 us (0.38)
  waiting for transfers between devices: 127 us -> 0 us
  Pallas kernels: 0 us -> 113 us
  blocking collectives: 107 us -> 0 us
  local copies, waits for them, and re-layouts: 23.9 us -> 3.04 us
  matrix products: 19.2 us -> 0 us
  other arithmetic: 13.8 us -> 0 us
  between operations: 14 us -> 0.64 us
  starting transfers between devices: 5.87 us -> 0 us
    pallas_call x0 -> x1, Pallas kernels: none -> 113 us  [per_device(): pl.pallas_call(kernel, out_shape=(jax.ShapeDtypeStruct((MICRO, ROWS, PART...]
    reduce_scatter x1 -> x0, waiting for transfers between devices: 81.5 us -> none  [per_device(): lax.psum_scatter(partial_value, 'tensor', scatter_dimension=3, tiled=True)]
    all_gather x3 -> x0, blocking collectives: 53.9 us -> none  [the longest x1 29.4 us: per_device(): piece = lax.all_gather(kv_pair, 'expert', axis=1, tiled=True)]
    all_to_all x1 -> x0, blocking collectives: 52.9 us -> none  [per_device(): lax.all_to_all(outgoing, 'expert', split_axis=1, concat_axis=1, tiled=True)]
    all_gather x2 -> x0, waiting for transfers between devices: 19.3 us -> none  [the longest x1 16.9 us: per_device(): lax.all_gather(local_rows, 'tensor', axis=2, tiled=True)]
    dot_general x9 -> x0, matrix products: 19.2 us -> none  [the longest x1 5.59 us: per_device(): jnp.dot(hidden, down_weight, preferred_element_type=jnp.float32)]
    all_to_all x1 -> x0, waiting for transfers between devices: 14.4 us -> none  [per_device(): lax.all_to_all(summed, 'expert', split_axis=1, concat_axis=1, tiled=True)]
    ppermute x1 -> x0, waiting for transfers between devices: 10.8 us -> none  [shifted(): return lax.ppermute(x, axis, [(i, (i + by) % size) for i in range(size)])]
  transfers between devices with their start and end apart: 5 -> 0, of which waited for: 5 -> 0; matrix products, arithmetic and copies ran while one was open for 4% -> 0% of each run, Pallas kernels for 0% -> 0%
where the time goes in v1:
time: 117 us
  Pallas kernels  113 us (97%)
  local copies, waits for them, and re-layouts  3.04 us (3%)
    pallas_call x1, Pallas kernels, per_device(): pl.pallas_call(kernel, out_shape=(jax.ShapeDtypeStruct((MICRO, ROWS, PART...  113 us
    unnamed x2, local copies, waits for them, and re-layouts  3.04 us

profile of v1, /device:TPU:32, one launch (start us, length us, event | category | flops | bytes accessed | tf_op | source)
XLA Modules:
  0.0 117.1 jit_solution(276267839415255615)
XLA Ops:
  0.6 113.4 %shard_map.122 = (bf16[2,64,1024]{2,1,0:T(8,128)(2,1)}, bf16[2,64,128]{2,1,0:T(8,128)(2,1)}) custom-call(bf16[2,64,1024]{2,1,0:T(8,128)(2,1)} %bitcast.21, s32[2,2,64]{2,1,0:T(2,128)} %bitcast.22, f32[2,2,64]{2,1,0:T(2,128)} %bitcast.23, bf16[1,1024]{1,0:T(2,128)(2,1)} %mgain_hbm.1, bf16[1,1024]{1,0:T(2,128)(2,1)} %again_hbm.1, bf16[4096,384]{1,0:T(8,128)(2,1)} %bitcast.16, ...), custom_call_target="tpu_custom_call" | custom-call | flops 5299999744 | bytes 13000000 | tf_op jit(solution)/shard_map/pallas_call | solution.py:578
  114.1 1.7 %copy.15 = bf16[1,2,64,1024]{3,2,1,0:T(8,128)(2,1)} copy(bf16[1,2,64,1024]{3,2,1,0:T(8,128)(2,1)} %bitcast.14) | data formatting | bytes 524288
  115.7 1.4 %copy.16 = bf16[1,2,64,128]{3,2,1,0:T(8,128)(2,1)} copy(bf16[1,2,64,128]{3,2,1,0:T(8,128)(2,1)} %bitcast.15) | data formatting | bytes 65536

commit v2 on v1

--- a/solution.py
+++ b/solution.py
@@ -24,10 +24,12 @@
 HALF = SLOTS // 2
 CUTS = 2
 WIDE = PART // CUTS
+SHARE = 384
+KEEP = PART - SHARE
 FF = 384
 LENGTH = EXPERTS * ROWS
 RIGHT, OPPOSITE, LEFT = 1, 2, 3
-SEMAPHORES = 160
+SEMAPHORES = 136
 
 
 def rope_table(length):
@@ -124,7 +126,7 @@
     wg_hbm, wu_hbm, wd_hbm, wq_hbm, wkv_hbm, rope_hbm,
     moe_out, context_out,
     stream, ids, gates, mgain, again, w13, wd, wqkv, wkv, rope,
-    ssq, gains, out, x, acc, hidden,
+    ssq, gains, raw, out, x, out_all, x_all, rates_out, rates_in, acc, hidden,
     opp, going_r, going_l, part_r, part_l, own, opp_l, opp_r, sum_l, sum_r,
     steps_r, steps_l, steps_from_r, steps_from_l, more_r, more_l, more_from_r, more_from_l,
     eo, ret, mixed, rows_in, kv_own, kv_in, context,
@@ -181,7 +183,9 @@
 
     value = stream[...].reshape(MICRO * ROWS, PART).astype(F32)
     ssq[0] = jnp.broadcast_to(flipped(jnp.sum(value * value, axis=1, keepdims=True)), (8, MICRO * ROWS))
-    gains[0] = jnp.broadcast_to(again[...], (16, PART))
+    gains[0, :8] = jnp.broadcast_to(mgain[...], (8, PART))
+    gains[0, 8:] = jnp.broadcast_to(again[...], (8, PART))
+    raw[0] = stream[:, :, KEEP:]
 
     pl.semaphore_wait(barrier, len(peers))
 
@@ -191,12 +195,11 @@
             msg.send(buffer.at[0], buffer.at[rel], leaving, coming, tensor=other)
         return coming
 
-    msg.wait(to_tensor_peers(ssq))
-    total = (ssq[0, 0:1, :] + ssq[1, 0:1, :]) + (ssq[2, 0:1, :] + ssq[3, 0:1, :])
-    scales = flipped(lax.rsqrt(total * (1.0 / (4 * PART)) + EPS))
-
     out_leave = [msg.leaving(out.at[m, 1:]) for m in range(MICRO)]
     out_come = [[None] + [msg.coming(x.at[m, 0, o]) for o in range(1, EXPERTS)] for m in range(MICRO)]
+    all_leave = [msg.leaving(out_all.at[m, 1:]) for m in range(MICRO)]
+    all_come = [msg.coming(x_all.at[m, 1:]) for m in range(MICRO)]
+    rates_leave, rates_come = msg.leaving(rates_out.at[1:]), msg.coming(rates_in.at[1:])
     x_leave_r = [msg.leaving(x.at[m, 0]) for m in range(MICRO)]
     x_leave_l = [msg.leaving(x.at[m, 0]) for m in range(MICRO)]
     near = EXPERTS // 2
@@ -213,16 +216,41 @@
     ahead_come_r = [msg.coming(x.at[m, OPPOSITE, :near]) for m in range(MICRO)]
     ahead_come_l = [msg.coming(x.at[m, OPPOSITE, near:]) for m in range(MICRO)]
 
-    def place_rows(m):
-        scale = scales[m * ROWS : (m + 1) * ROWS]
-        normed = (stream[m].astype(F32) * scale * mgain[...].astype(F32)).astype(BF16)
-        block = dot(chosen[m][0] + chosen[m][1], normed).astype(BF16).reshape(EXPERTS, CAP, PART)
+    placing = [chosen[m][0] + chosen[m][1] for m in range(MICRO)]
+
+    def dispatch(m):
+        block = dot(placing[m], stream[m, :, :KEEP]).astype(BF16).reshape(EXPERTS, CAP, KEEP)
         x[m, 0, 0] = block[0]
         out[m] = block
-
-    def dispatch(m):
         for o in range(1, EXPERTS):
             msg.send(out.at[m, o], x.at[m, 0, o], out_leave[m], out_come[m][o], expert=peer[o])
+
+    def dispatch_all(m):
+        for rel in range(4):
+            at = slice(rel * SHARE, (rel + 1) * SHARE)
+            block = dot(placing[m], raw[rel, m]).astype(BF16).reshape(EXPERTS, CAP, SHARE)
+            x_all[m, 0, :, at] = block[0]
+            out_all[m, :, :, at] = block
+        for o in range(1, EXPERTS):
+            msg.send(out_all.at[m, o], x_all.at[m, o], all_leave[m], all_come[m], expert=peer[o])
+
+    def dispatch_rates():
+        total = (ssq[0, 0:1, :] + ssq[1, 0:1, :]) + (ssq[2, 0:1, :] + ssq[3, 0:1, :])
+        scales = lax.rsqrt(total * (1.0 / (4 * PART)) + EPS)
+        rates_out[...] = jnp.zeros(rates_out.shape, F32)
+        for m in range(MICRO):
+            scale = scales[:, m * ROWS : (m + 1) * ROWS]
+            rate = jnp.sum(placing[m].astype(F32) * scale, axis=1, keepdims=True)
+            for o in range(EXPERTS):
+                rates_out[o, m : m + 1, :CAP] = flipped(rate[o * CAP : (o + 1) * CAP])
+        rates_in[0] = rates_out[0]
+        for o in range(1, EXPERTS):
+            msg.send(rates_out.at[o], rates_in.at[o], rates_leave, rates_come, expert=peer[o])
+
+    def rates_of(m):
+        return jnp.concatenate(
+            [flipped(rates_in[o, m : m + 1, :CAP]) for o in range(EXPERTS)], axis=0
+        )
 
     def gather_send(m, pieces):
         for o in pieces:
@@ -239,12 +267,26 @@
             msg.wait(x_come_l[m][o])
             msg.send(x.at[m, LEFT, o], x.at[m, OPPOSITE, o], ahead_leave_l[m], ahead_come_l[m], tensor=left)
 
-    def quarter(rel):
-        return pl.ds(pl.multiple_of(lax.rem(t + 4 - rel, 4) * PART, PART), PART)
+    def columns_of(rel, first, width):
+        return pl.ds(pl.multiple_of(lax.rem(t + 4 - rel, 4) * PART + first, HS), width)
+
+    def normed_rows(rows, rate, gain):
+        return (rows.astype(F32) * rate * gain.astype(F32)).astype(BF16)
 
     def expert_in(m, rel):
-        value = dot(x[m, rel].reshape(SLOTS, PART), w13[quarter(rel), :])
+        rows = x[m, rel].reshape(SLOTS, KEEP)
+        normed = normed_rows(rows, rates_of(m), gains[rel, 0:1, :KEEP])
+        value = dot(normed, w13[columns_of(rel, 0, KEEP), :])
         acc[...] = value if rel == 0 else acc[...] + value
+
+    def expert_in_all(m):
+        value = None
+        for rel in range(4):
+            rows = x_all[m, :, :, rel * SHARE : (rel + 1) * SHARE].reshape(SLOTS, SHARE)
+            normed = normed_rows(rows, rates_of(m), gains[rel, 0:1, KEEP:])
+            term = dot(normed, w13[columns_of(rel, KEEP, SHARE), :])
+            value = term if value is None else value + term
+        acc[...] += value
 
     def activate(m):
         gated, lifted = acc[:, :FF], acc[:, FF:]
@@ -356,35 +398,15 @@
         )
         moe_writes[-1].start()
 
-    half = ROWS // 2
-    rows_leave_r, rows_leave_l = (
-        [msg.leaving(rows_in.at[m, 0]) for m in range(MICRO)] for _ in range(2)
-    )
-    rows_ahead_r = [msg.leaving(rows_in.at[m, RIGHT, :, :half]) for m in range(MICRO)]
-    rows_ahead_l = [msg.leaving(rows_in.at[m, LEFT, :, half:]) for m in range(MICRO)]
-    rows_come_r, rows_come_l = (
-        [[msg.coming(rows_in.at[m, rel, c]) for c in range(CUTS)] for m in range(MICRO)]
-        for rel in (RIGHT, LEFT)
-    )
-    rows_far_r = [[msg.coming(rows_in.at[m, OPPOSITE, c, :half]) for c in range(CUTS)] for m in range(MICRO)]
-    rows_far_l = [[msg.coming(rows_in.at[m, OPPOSITE, c, half:]) for c in range(CUTS)] for m in range(MICRO)]
+    rows_leave = [msg.leaving(rows_in.at[m, 1:]) for m in range(MICRO)]
+    rows_come = [[msg.coming(rows_in.at[m, 1:, c]) for c in range(CUTS)] for m in range(MICRO)]
 
     def rows_send(m, c):
         msg.wait(shift_come[m][c])
-        msg.send(rows_in.at[m, 0, c], rows_in.at[m, RIGHT, c], rows_leave_r[m], rows_come_r[m][c], tensor=right)
-        msg.send(rows_in.at[m, 0, c], rows_in.at[m, LEFT, c], rows_leave_l[m], rows_come_l[m][c], tensor=left)
-
-    def rows_forward(m, c):
-        msg.wait(rows_come_r[m][c])
-        msg.send(
-            rows_in.at[m, RIGHT, c, :half], rows_in.at[m, OPPOSITE, c, :half],
-            rows_ahead_r[m], rows_far_r[m][c], tensor=right,
-        )
-        msg.wait(rows_come_l[m][c])
-        msg.send(
-            rows_in.at[m, LEFT, c, half:], rows_in.at[m, OPPOSITE, c, half:],
-            rows_ahead_l[m], rows_far_l[m][c], tensor=left,
-        )
+        for rel, other in ((OPPOSITE, opposite), (RIGHT, right), (LEFT, left)):
+            msg.send(
+                rows_in.at[m, 0, c], rows_in.at[m, rel, c], rows_leave[m], rows_come[m][c], tensor=other
+            )
 
     kv_leave = [msg.leaving(kv_in.at[m, 1:]) for m in range(MICRO)]
     kv_come = [msg.coming(kv_in.at[m, 1:]) for m in range(MICRO)]
@@ -395,8 +417,7 @@
 
     def project(m):
         for c in range(CUTS):
-            msg.wait(rows_far_r[m][c])
-            msg.wait(rows_far_l[m][c])
+            msg.wait(rows_come[m][c])
         total = None
         for rel in range(4):
             for c in range(CUTS):
@@ -407,7 +428,7 @@
         result = None
         for rel in range(4):
             for c in range(CUTS):
-                gain = gains[rel, 0:1, c * WIDE : (c + 1) * WIDE].astype(F32)
+                gain = gains[rel, 8:9, c * WIDE : (c + 1) * WIDE].astype(F32)
                 normed = (rows_in[m, rel, c].astype(F32) * scale * gain).astype(BF16)
                 at = pl.multiple_of(lax.rem(t + 4 - rel, 4) * PART + c * WIDE, WIDE)
                 term = dot(normed, wqkv[pl.ds(at, WIDE), :])
@@ -453,16 +474,23 @@
 
         lax.fori_loop(0, wkv.shape[0] // step, body, 0)
 
-    place_rows(0)
+    raw_come = to_tensor_peers(raw)
     dispatch(0)
+    ssq_come = to_tensor_peers(ssq)
     gather_send(0, [0])
-    place_rows(1)
-    gather_send(0, [1, 2, 3, 4])
+    gains_come = to_tensor_peers(gains)
     dispatch(1)
-    gather_send(0, [5, 6, 7])
-    gains_come = to_tensor_peers(gains)
+    msg.wait(ssq_come)
+    dispatch_rates()
+    gather_send(0, [1, 2, 3])
+    msg.wait(raw_come)
+    dispatch_all(0)
+    gather_send(0, [4, 5, 6, 7])
+    dispatch_all(1)
     for load in loads[5:]:
         load.wait()
+    msg.wait(rates_come)
+    msg.wait(gains_come)
     expert_in(0, 0)
     gather_forward(0)
     gather_send(1, range(EXPERTS))
@@ -474,6 +502,8 @@
     msg.wait(ahead_come_r[0])
     msg.wait(ahead_come_l[0])
     expert_in(0, OPPOSITE)
+    msg.wait(all_come[0])
+    expert_in_all(0)
     activate(0)
     for c in range(CUTS):
         send_opposite(0, c)
@@ -491,6 +521,8 @@
     msg.wait(ahead_come_r[1])
     msg.wait(ahead_come_l[1])
     expert_in(1, OPPOSITE)
+    msg.wait(all_come[1])
+    expert_in_all(1)
     activate(1)
     send_opposite(1, 0)
     send_direct(1, 0)
@@ -508,17 +540,12 @@
     rows_send(0, 0)
     rows_send(0, 1)
     sum_last(1, 1)
-    msg.wait(gains_come)
-    rows_forward(0, 0)
-    rows_forward(0, 1)
     combine(1, 0)
     query0 = project(0)
     combine(1, 1)
     rows_send(1, 0)
     rows_send(1, 1)
     attend(0, query0)
-    rows_forward(1, 0)
-    rows_forward(1, 1)
     query1 = project(1)
     attend(1, query1)
 
@@ -550,8 +577,13 @@
         ((ROWS, 2 * HS), F32),
         ((4, 8, MICRO * ROWS), F32),
         ((4, 16, PART), BF16),
-        ((MICRO, EXPERTS, CAP, PART), BF16),
-        ((MICRO, 4, EXPERTS, CAP, PART), BF16),
+        ((4, MICRO, ROWS, SHARE), BF16),
+        ((MICRO, EXPERTS, CAP, KEEP), BF16),
+        ((MICRO, 4, EXPERTS, CAP, KEEP), BF16),
+        ((MICRO, EXPERTS, CAP, 4 * SHARE), BF16),
+        ((MICRO, EXPERTS, CAP, 4 * SHARE), BF16),
+        ((EXPERTS, 8, HS), F32),
+        ((EXPERTS, 8, HS), F32),
         ((SLOTS, 2 * FF), F32),
         ((MICRO, SLOTS, FF), BF16),
         (slots_cut, I16),

time: 117 us -> 102 us (0.87)
  Pallas kernels: 113 us -> 98.6 us
    pallas_call x1, Pallas kernels: 113 us -> 98.6 us  [per_device(): pl.pallas_call(kernel, out_shape=(jax.ShapeDtypeStruct((MICRO, ROWS, PART...]
where the time goes in v2:
time: 102 us
  Pallas kernels  98.6 us (97%)
  local copies, waits for them, and re-layouts  3.04 us (3%)
    pallas_call x1, Pallas kernels, per_device(): pl.pallas_call(kernel, out_shape=(jax.ShapeDtypeStruct((MICRO, ROWS, PART...  98.6 us
    unnamed x2, local copies, waits for them, and re-layouts  3.04 us

profile of v2, /device:TPU:32, one launch (start us, length us, event | category | flops | bytes accessed | tf_op | source)
XLA Modules:
  0.0 102.3 jit_solution(5314060700851494692)
XLA Ops:
  0.6 98.6 %shard_map.122 = (bf16[2,64,1024]{2,1,0:T(8,128)(2,1)}, bf16[2,64,128]{2,1,0:T(8,128)(2,1)}) custom-call(bf16[2,64,1024]{2,1,0:T(8,128)(2,1)} %bitcast.21, s32[2,2,64]{2,1,0:T(2,128)} %bitcast.22, f32[2,2,64]{2,1,0:T(2,128)} %bitcast.23, bf16[1,1024]{1,0:T(2,128)(2,1)} %mgain_hbm.1, bf16[1,1024]{1,0:T(2,128)(2,1)} %again_hbm.1, bf16[4096,384]{1,0:T(8,128)(2,1)} %bitcast.16, ...), custom_call_target="tpu_custom_call" | custom-call | flops 5299999744 | bytes 13000000 | tf_op jit(solution)/shard_map/pallas_call | solution.py:610
  99.2 1.7 %copy.15 = bf16[1,2,64,1024]{3,2,1,0:T(8,128)(2,1)} copy(bf16[1,2,64,1024]{3,2,1,0:T(8,128)(2,1)} %bitcast.14) | data formatting | bytes 524288
  100.9 1.4 %copy.16 = bf16[1,2,64,128]{3,2,1,0:T(8,128)(2,1)} copy(bf16[1,2,64,128]{3,2,1,0:T(8,128)(2,1)} %bitcast.15) | data formatting | bytes 65536

commit v3 on v2

--- a/solution.py
+++ b/solution.py
@@ -24,12 +24,13 @@
 HALF = SLOTS // 2
 CUTS = 2
 WIDE = PART // CUTS
-SHARE = 384
-KEEP = PART - SHARE
+SHARE = (384, 768)
+KEEP = tuple(PART - share for share in SHARE)
 FF = 384
 LENGTH = EXPERTS * ROWS
 RIGHT, OPPOSITE, LEFT = 1, 2, 3
-SEMAPHORES = 136
+SEMAPHORES = 138
+ORDER = (0, 4, 1, 5, 2, 6, 3, 7)
 
 
 def rope_table(length):
@@ -126,7 +127,7 @@
     wg_hbm, wu_hbm, wd_hbm, wq_hbm, wkv_hbm, rope_hbm,
     moe_out, context_out,
     stream, ids, gates, mgain, again, w13, wd, wqkv, wkv, rope,
-    ssq, gains, raw, out, x, out_all, x_all, rates_out, rates_in, acc, hidden,
+    ssq, gains, raw0, raw1, out0, out1, x0, x1, out_all0, out_all1, x_all0, x_all1, rates_out, rates_in, acc, hidden,
     opp, going_r, going_l, part_r, part_l, own, opp_l, opp_r, sum_l, sum_r,
     steps_r, steps_l, steps_from_r, steps_from_l, more_r, more_l, more_from_r, more_from_l,
     eo, ret, mixed, rows_in, kv_own, kv_in, context,
@@ -137,6 +138,8 @@
     after, before = lax.rem(p + 1, 8), lax.rem(p + 7, 8)
     peer = [lax.rem(e + o, EXPERTS) for o in range(EXPERTS)]
     msg = Messages(sems)
+    raw, out, x = (raw0, raw1), (out0, out1), (x0, x1)
+    out_all, x_all = (out_all0, out_all1), (x_all0, x_all1)
 
     here = pl.ds(pl.multiple_of(e * ROWS, ROWS), ROWS)
     loads = [
@@ -185,7 +188,8 @@
     ssq[0] = jnp.broadcast_to(flipped(jnp.sum(value * value, axis=1, keepdims=True)), (8, MICRO * ROWS))
     gains[0, :8] = jnp.broadcast_to(mgain[...], (8, PART))
     gains[0, 8:] = jnp.broadcast_to(again[...], (8, PART))
-    raw[0] = stream[:, :, KEEP:]
+    for m in range(MICRO):
+        raw[m][0] = stream[m, :, KEEP[m] :]
 
     pl.semaphore_wait(barrier, len(peers))
 
@@ -195,44 +199,44 @@
             msg.send(buffer.at[0], buffer.at[rel], leaving, coming, tensor=other)
         return coming
 
-    out_leave = [msg.leaving(out.at[m, 1:]) for m in range(MICRO)]
-    out_come = [[None] + [msg.coming(x.at[m, 0, o]) for o in range(1, EXPERTS)] for m in range(MICRO)]
-    all_leave = [msg.leaving(out_all.at[m, 1:]) for m in range(MICRO)]
-    all_come = [msg.coming(x_all.at[m, 1:]) for m in range(MICRO)]
+    out_leave = [msg.leaving(out[m].at[1:]) for m in range(MICRO)]
+    out_come = [[None] + [msg.coming(x[m].at[0, o]) for o in range(1, EXPERTS)] for m in range(MICRO)]
+    all_leave = [msg.leaving(out_all[m].at[1:]) for m in range(MICRO)]
+    all_come = [msg.coming(x_all[m].at[1:]) for m in range(MICRO)]
     rates_leave, rates_come = msg.leaving(rates_out.at[1:]), msg.coming(rates_in.at[1:])
-    x_leave_r = [msg.leaving(x.at[m, 0]) for m in range(MICRO)]
-    x_leave_l = [msg.leaving(x.at[m, 0]) for m in range(MICRO)]
+    x_leave_r = [msg.leaving(x[m].at[0]) for m in range(MICRO)]
+    x_leave_l = [msg.leaving(x[m].at[0]) for m in range(MICRO)]
     near = EXPERTS // 2
     x_come_r = [
-        [msg.coming(x.at[m, RIGHT, o]) for o in range(near)] + [msg.coming(x.at[m, RIGHT, near:])] * near
+        [msg.coming(x[m].at[RIGHT, o]) for o in range(near)] + [msg.coming(x[m].at[RIGHT, near:])] * near
         for m in range(MICRO)
     ]
     x_come_l = [
-        [msg.coming(x.at[m, LEFT, :near])] * near + [msg.coming(x.at[m, LEFT, o]) for o in range(near, EXPERTS)]
+        [msg.coming(x[m].at[LEFT, :near])] * near + [msg.coming(x[m].at[LEFT, o]) for o in range(near, EXPERTS)]
         for m in range(MICRO)
     ]
-    ahead_leave_r = [msg.leaving(x.at[m, RIGHT, :near]) for m in range(MICRO)]
-    ahead_leave_l = [msg.leaving(x.at[m, LEFT, near:]) for m in range(MICRO)]
-    ahead_come_r = [msg.coming(x.at[m, OPPOSITE, :near]) for m in range(MICRO)]
-    ahead_come_l = [msg.coming(x.at[m, OPPOSITE, near:]) for m in range(MICRO)]
+    ahead_leave_r = [msg.leaving(x[m].at[RIGHT, :near]) for m in range(MICRO)]
+    ahead_leave_l = [msg.leaving(x[m].at[LEFT, near:]) for m in range(MICRO)]
+    ahead_come_r = [msg.coming(x[m].at[OPPOSITE, :near]) for m in range(MICRO)]
+    ahead_come_l = [msg.coming(x[m].at[OPPOSITE, near:]) for m in range(MICRO)]
 
     placing = [chosen[m][0] + chosen[m][1] for m in range(MICRO)]
 
     def dispatch(m):
-        block = dot(placing[m], stream[m, :, :KEEP]).astype(BF16).reshape(EXPERTS, CAP, KEEP)
-        x[m, 0, 0] = block[0]
-        out[m] = block
-        for o in range(1, EXPERTS):
-            msg.send(out.at[m, o], x.at[m, 0, o], out_leave[m], out_come[m][o], expert=peer[o])
+        block = dot(placing[m], stream[m, :, : KEEP[m]]).astype(BF16).reshape(EXPERTS, CAP, KEEP[m])
+        x[m][0, 0] = block[0]
+        out[m][...] = block
+        for o in ORDER[1:]:
+            msg.send(out[m].at[o], x[m].at[0, o], out_leave[m], out_come[m][o], expert=peer[o])
 
     def dispatch_all(m):
         for rel in range(4):
-            at = slice(rel * SHARE, (rel + 1) * SHARE)
-            block = dot(placing[m], raw[rel, m]).astype(BF16).reshape(EXPERTS, CAP, SHARE)
-            x_all[m, 0, :, at] = block[0]
-            out_all[m, :, :, at] = block
+            at = slice(rel * SHARE[m], (rel + 1) * SHARE[m])
+            block = dot(placing[m], raw[m][rel]).astype(BF16).reshape(EXPERTS, CAP, SHARE[m])
+            x_all[m][0, :, at] = block[0]
+            out_all[m][:, :, at] = block
         for o in range(1, EXPERTS):
-            msg.send(out_all.at[m, o], x_all.at[m, o], all_leave[m], all_come[m], expert=peer[o])
+            msg.send(out_all[m].at[o], x_all[m].at[o], all_leave[m], all_come[m], expert=peer[o])
 
     def dispatch_rates():
         total = (ssq[0, 0:1, :] + ssq[1, 0:1, :]) + (ssq[2, 0:1, :] + ssq[3, 0:1, :])
@@ -256,16 +260,16 @@
         for o in pieces:
             if o > 0:
                 msg.wait(out_come[m][o])
-            msg.send(x.at[m, 0, o], x.at[m, RIGHT, o], x_leave_r[m], x_come_r[m][o], tensor=right)
-            msg.send(x.at[m, 0, o], x.at[m, LEFT, o], x_leave_l[m], x_come_l[m][o], tensor=left)
+            msg.send(x[m].at[0, o], x[m].at[RIGHT, o], x_leave_r[m], x_come_r[m][o], tensor=right)
+            msg.send(x[m].at[0, o], x[m].at[LEFT, o], x_leave_l[m], x_come_l[m][o], tensor=left)
 
     def gather_forward(m):
         for i in range(near):
             msg.wait(x_come_r[m][i])
-            msg.send(x.at[m, RIGHT, i], x.at[m, OPPOSITE, i], ahead_leave_r[m], ahead_come_r[m], tensor=right)
+            msg.send(x[m].at[RIGHT, i], x[m].at[OPPOSITE, i], ahead_leave_r[m], ahead_come_r[m], tensor=right)
             o = i + near
             msg.wait(x_come_l[m][o])
-            msg.send(x.at[m, LEFT, o], x.at[m, OPPOSITE, o], ahead_leave_l[m], ahead_come_l[m], tensor=left)
+            msg.send(x[m].at[LEFT, o], x[m].at[OPPOSITE, o], ahead_leave_l[m], ahead_come_l[m], tensor=left)
 
     def columns_of(rel, first, width):
         return pl.ds(pl.multiple_of(lax.rem(t + 4 - rel, 4) * PART + first, HS), width)
@@ -274,17 +278,17 @@
         return (rows.astype(F32) * rate * gain.astype(F32)).astype(BF16)
 
     def expert_in(m, rel):
-        rows = x[m, rel].reshape(SLOTS, KEEP)
-        normed = normed_rows(rows, rates_of(m), gains[rel, 0:1, :KEEP])
-        value = dot(normed, w13[columns_of(rel, 0, KEEP), :])
+        rows = x[m][rel].reshape(SLOTS, KEEP[m])
+        normed = normed_rows(rows, rates_of(m), gains[rel, 0:1, : KEEP[m]])
+        value = dot(normed, w13[columns_of(rel, 0, KEEP[m]), :])
         acc[...] = value if rel == 0 else acc[...] + value
 
     def expert_in_all(m):
         value = None
         for rel in range(4):
-            rows = x_all[m, :, :, rel * SHARE : (rel + 1) * SHARE].reshape(SLOTS, SHARE)
-            normed = normed_rows(rows, rates_of(m), gains[rel, 0:1, KEEP:])
-            term = dot(normed, w13[columns_of(rel, KEEP, SHARE), :])
+            rows = x_all[m][:, :, rel * SHARE[m] : (rel + 1) * SHARE[m]].reshape(SLOTS, SHARE[m])
+            normed = normed_rows(rows, rates_of(m), gains[rel, 0:1, KEEP[m] :])
+            term = dot(normed, w13[columns_of(rel, KEEP[m], SHARE[m]), :])
             value = term if value is None else value + term
         acc[...] += value
 
@@ -474,27 +478,28 @@
 
         lax.fori_loop(0, wkv.shape[0] // step, body, 0)
 
-    raw_come = to_tensor_peers(raw)
+    raw_come = [to_tensor_peers(raw[0])]
     dispatch(0)
+    gather_send(0, [0])
+    dispatch(1)
     ssq_come = to_tensor_peers(ssq)
-    gather_send(0, [0])
+    raw_come.append(to_tensor_peers(raw[1]))
     gains_come = to_tensor_peers(gains)
-    dispatch(1)
+    msg.wait(raw_come[0])
+    dispatch_all(0)
+    gather_send(0, ORDER[1:5])
     msg.wait(ssq_come)
     dispatch_rates()
-    gather_send(0, [1, 2, 3])
-    msg.wait(raw_come)
-    dispatch_all(0)
-    gather_send(0, [4, 5, 6, 7])
+    gather_send(0, ORDER[5:])
+    gather_forward(0)
+    msg.wait(raw_come[1])
     dispatch_all(1)
+    gather_send(1, ORDER)
     for load in loads[5:]:
         load.wait()
     msg.wait(rates_come)
     msg.wait(gains_come)
     expert_in(0, 0)
-    gather_forward(0)
-    gather_send(1, range(EXPERTS))
-    split_weights()
     msg.wait(x_come_r[0][near])
     expert_in(0, RIGHT)
     msg.wait(x_come_l[0][0])
@@ -508,12 +513,12 @@
     for c in range(CUTS):
         send_opposite(0, c)
         send_direct(0, c)
+    gather_forward(1)
     for c in range(CUTS):
         own[0, c] = part(0, c, 0)
+        sum_middle(0, c)
     expert_in(1, 0)
-    gather_forward(1)
-    for c in range(CUTS):
-        sum_middle(0, c)
+    split_weights()
     msg.wait(x_come_r[1][near])
     expert_in(1, RIGHT)
     msg.wait(x_come_l[1][0])
@@ -577,11 +582,10 @@
         ((ROWS, 2 * HS), F32),
         ((4, 8, MICRO * ROWS), F32),
         ((4, 16, PART), BF16),
-        ((4, MICRO, ROWS, SHARE), BF16),
-        ((MICRO, EXPERTS, CAP, KEEP), BF16),
-        ((MICRO, 4, EXPERTS, CAP, KEEP), BF16),
-        ((MICRO, EXPERTS, CAP, 4 * SHARE), BF16),
-        ((MICRO, EXPERTS, CAP, 4 * SHARE), BF16),
+        *(((4, ROWS, SHARE[m]), BF16) for m in range(MICRO)),
+        *(((EXPERTS, CAP, KEEP[m]), BF16) for m in range(MICRO)),
+        *(((4, EXPERTS, CAP, KEEP[m]), BF16) for m in range(MICRO)),
+        *(((EXPERTS, CAP, 4 * SHARE[m]), BF16) for m in (0, 1, 0, 1)),
         ((EXPERTS, 8, HS), F32),
         ((EXPERTS, 8, HS), F32),
         ((SLOTS, 2 * FF), F32),

time: 102 us -> 99.8 us (0.978)
  Pallas kernels: 98.6 us -> 95.9 us
    pallas_call x1, Pallas kernels: 98.6 us -> 95.9 us  [per_device(): pl.pallas_call(kernel, out_shape=(jax.ShapeDtypeStruct((MICRO, ROWS, PART...]
where the time goes in v3:
time: 99.8 us; the launch traced here: 99.6 us
  Pallas kernels  95.9 us (96%)
  local copies, waits for them, and re-layouts  3.04 us (3%)
    pallas_call x1, Pallas kernels, per_device(): pl.pallas_call(kernel, out_shape=(jax.ShapeDtypeStruct((MICRO, ROWS, PART...  95.9 us
    unnamed x2, local copies, waits for them, and re-layouts  3.04 us

profile of v3, /device:TPU:32, one launch (start us, length us, event | category | flops | bytes accessed | tf_op | source)
XLA Modules:
  0.0 99.6 jit_solution(5809135140259022613)
XLA Ops:
  0.6 95.9 %shard_map.122 = (bf16[2,64,1024]{2,1,0:T(8,128)(2,1)}, bf16[2,64,128]{2,1,0:T(8,128)(2,1)}) custom-call(bf16[2,64,1024]{2,1,0:T(8,128)(2,1)} %bitcast.21, s32[2,2,64]{2,1,0:T(2,128)} %bitcast.22, f32[2,2,64]{2,1,0:T(2,128)} %bitcast.23, bf16[1,1024]{1,0:T(2,128)(2,1)} %mgain_hbm.1, bf16[1,1024]{1,0:T(2,128)(2,1)} %again_hbm.1, bf16[4096,384]{1,0:T(8,128)(2,1)} %bitcast.16, ...), custom_call_target="tpu_custom_call" | custom-call | flops 5299999744 | bytes 13000000 | tf_op jit(solution)/shard_map/pallas_call | solution.py:614
  96.6 1.7 %copy.15 = bf16[1,2,64,1024]{3,2,1,0:T(8,128)(2,1)} copy(bf16[1,2,64,1024]{3,2,1,0:T(8,128)(2,1)} %bitcast.14) | data formatting | bytes 524288
  98.2 1.4 %copy.16 = bf16[1,2,64,128]{3,2,1,0:T(8,128)(2,1)} copy(bf16[1,2,64,128]{3,2,1,0:T(8,128)(2,1)} %bitcast.15) | data formatting | bytes 65536

commit v4 on v3

--- a/solution.py
+++ b/solution.py
@@ -29,7 +29,7 @@
 FF = 384
 LENGTH = EXPERTS * ROWS
 RIGHT, OPPOSITE, LEFT = 1, 2, 3
-SEMAPHORES = 138
+SEMAPHORES = 144
 ORDER = (0, 4, 1, 5, 2, 6, 3, 7)
 
 
@@ -202,7 +202,8 @@
     out_leave = [msg.leaving(out[m].at[1:]) for m in range(MICRO)]
     out_come = [[None] + [msg.coming(x[m].at[0, o]) for o in range(1, EXPERTS)] for m in range(MICRO)]
     all_leave = [msg.leaving(out_all[m].at[1:]) for m in range(MICRO)]
-    all_come = [msg.coming(x_all[m].at[1:]) for m in range(MICRO)]
+    shares = [[slice(r * SHARE[m], (r + 1) * SHARE[m]) for r in range(4)] for m in range(MICRO)]
+    all_come = [[msg.coming(x_all[m].at[1:, :, at]) for at in shares[m]] for m in range(MICRO)]
     rates_leave, rates_come = msg.leaving(rates_out.at[1:]), msg.coming(rates_in.at[1:])
     x_leave_r = [msg.leaving(x[m].at[0]) for m in range(MICRO)]
     x_leave_l = [msg.leaving(x[m].at[0]) for m in range(MICRO)]
@@ -230,13 +231,15 @@
             msg.send(out[m].at[o], x[m].at[0, o], out_leave[m], out_come[m][o], expert=peer[o])
 
     def dispatch_all(m):
-        for rel in range(4):
-            at = slice(rel * SHARE[m], (rel + 1) * SHARE[m])
+        for rel, at in enumerate(shares[m]):
             block = dot(placing[m], raw[m][rel]).astype(BF16).reshape(EXPERTS, CAP, SHARE[m])
             x_all[m][0, :, at] = block[0]
             out_all[m][:, :, at] = block
-        for o in range(1, EXPERTS):
-            msg.send(out_all[m].at[o], x_all[m].at[o], all_leave[m], all_come[m], expert=peer[o])
+            for o in range(1, EXPERTS):
+                msg.send(
+                    out_all[m].at[o, :, at], x_all[m].at[o, :, at],
+                    all_leave[m], all_come[m][rel], expert=peer[o],
+                )
 
     def dispatch_rates():
         total = (ssq[0, 0:1, :] + ssq[1, 0:1, :]) + (ssq[2, 0:1, :] + ssq[3, 0:1, :])
@@ -286,6 +289,7 @@
     def expert_in_all(m):
         value = None
         for rel in range(4):
+            msg.wait(all_come[m][rel])
             rows = x_all[m][:, :, rel * SHARE[m] : (rel + 1) * SHARE[m]].reshape(SLOTS, SHARE[m])
             normed = normed_rows(rows, rates_of(m), gains[rel, 0:1, KEEP[m] :])
             term = dot(normed, w13[columns_of(rel, KEEP[m], SHARE[m]), :])
@@ -507,7 +511,6 @@
     msg.wait(ahead_come_r[0])
     msg.wait(ahead_come_l[0])
     expert_in(0, OPPOSITE)
-    msg.wait(all_come[0])
     expert_in_all(0)
     activate(0)
     for c in range(CUTS):
@@ -526,7 +529,6 @@
     msg.wait(ahead_come_r[1])
     msg.wait(ahead_come_l[1])
     expert_in(1, OPPOSITE)
-    msg.wait(all_come[1])
     expert_in_all(1)
     activate(1)
     send_opposite(1, 0)

time: 99.8 us -> 101 us (1.012)
  Pallas kernels: 95.9 us -> 97.5 us
    pallas_call x1, Pallas kernels: 95.9 us -> 97.5 us  [per_device(): pl.pallas_call(kernel, out_shape=(jax.ShapeDtypeStruct((MICRO, ROWS, PART...]
where the time goes in v4:
time: 101 us
  Pallas kernels  97.5 us (97%)
  local copies, waits for them, and re-layouts  3.04 us (3%)
    pallas_call x1, Pallas kernels, per_device(): pl.pallas_call(kernel, out_shape=(jax.ShapeDtypeStruct((MICRO, ROWS, PART...  97.5 us
    unnamed x2, local copies, waits for them, and re-layouts  3.04 us

profile of v4, /device:TPU:32, one launch (start us, length us, event | category | flops | bytes accessed | tf_op | source)
XLA Modules:
  0.0 101.2 jit_solution(14489359805918108181)
XLA Ops:
  0.6 97.5 %shard_map.122 = (bf16[2,64,1024]{2,1,0:T(8,128)(2,1)}, bf16[2,64,128]{2,1,0:T(8,128)(2,1)}) custom-call(bf16[2,64,1024]{2,1,0:T(8,128)(2,1)} %bitcast.21, s32[2,2,64]{2,1,0:T(2,128)} %bitcast.22, f32[2,2,64]{2,1,0:T(2,128)} %bitcast.23, bf16[1,1024]{1,0:T(2,128)(2,1)} %mgain_hbm.1, bf16[1,1024]{1,0:T(2,128)(2,1)} %again_hbm.1, bf16[4096,384]{1,0:T(8,128)(2,1)} %bitcast.16, ...), custom_call_target="tpu_custom_call" | custom-call | flops 5299999744 | bytes 13000000 | tf_op jit(solution)/shard_map/pallas_call | solution.py:616
  98.2 1.7 %copy.15 = bf16[1,2,64,1024]{3,2,1,0:T(8,128)(2,1)} copy(bf16[1,2,64,1024]{3,2,1,0:T(8,128)(2,1)} %bitcast.14) | data formatting | bytes 524288
  99.8 1.4 %copy.16 = bf16[1,2,64,128]{3,2,1,0:T(8,128)(2,1)} copy(bf16[1,2,64,128]{3,2,1,0:T(8,128)(2,1)} %bitcast.15) | data formatting | bytes 65536

commit v5 on v3

--- a/solution.py
+++ b/solution.py
@@ -29,7 +29,7 @@
 FF = 384
 LENGTH = EXPERTS * ROWS
 RIGHT, OPPOSITE, LEFT = 1, 2, 3
-SEMAPHORES = 138
+SEMAPHORES = 140
 ORDER = (0, 4, 1, 5, 2, 6, 3, 7)
 
 
@@ -202,7 +202,10 @@
     out_leave = [msg.leaving(out[m].at[1:]) for m in range(MICRO)]
     out_come = [[None] + [msg.coming(x[m].at[0, o]) for o in range(1, EXPERTS)] for m in range(MICRO)]
     all_leave = [msg.leaving(out_all[m].at[1:]) for m in range(MICRO)]
-    all_come = [msg.coming(x_all[m].at[1:]) for m in range(MICRO)]
+    all_come = [
+        [msg.coming(x_all[m].at[1 : EXPERTS // 2]), msg.coming(x_all[m].at[EXPERTS // 2 :])]
+        for m in range(MICRO)
+    ]
     rates_leave, rates_come = msg.leaving(rates_out.at[1:]), msg.coming(rates_in.at[1:])
     x_leave_r = [msg.leaving(x[m].at[0]) for m in range(MICRO)]
     x_leave_l = [msg.leaving(x[m].at[0]) for m in range(MICRO)]
@@ -236,7 +239,7 @@
             x_all[m][0, :, at] = block[0]
             out_all[m][:, :, at] = block
         for o in range(1, EXPERTS):
-            msg.send(out_all[m].at[o], x_all[m].at[o], all_leave[m], all_come[m], expert=peer[o])
+            msg.send(out_all[m].at[o], x_all[m].at[o], all_leave[m], all_come[m][o // (EXPERTS // 2)], expert=peer[o])
 
     def dispatch_rates():
         total = (ssq[0, 0:1, :] + ssq[1, 0:1, :]) + (ssq[2, 0:1, :] + ssq[3, 0:1, :])
@@ -284,13 +287,19 @@
         acc[...] = value if rel == 0 else acc[...] + value
 
     def expert_in_all(m):
-        value = None
-        for rel in range(4):
-            rows = x_all[m][:, :, rel * SHARE[m] : (rel + 1) * SHARE[m]].reshape(SLOTS, SHARE[m])
-            normed = normed_rows(rows, rates_of(m), gains[rel, 0:1, KEEP[m] :])
-            term = dot(normed, w13[columns_of(rel, KEEP[m], SHARE[m]), :])
-            value = term if value is None else value + term
-        acc[...] += value
+        rate = rates_of(m)
+        for part_of, slots in enumerate((slice(0, HALF), slice(HALF, SLOTS))):
+            blocks = slice(part_of * (EXPERTS // 2), (part_of + 1) * (EXPERTS // 2))
+            msg.wait(all_come[m][part_of])
+            value = None
+            for rel in range(4):
+                rows = x_all[m][blocks, :, rel * SHARE[m] : (rel + 1) * SHARE[m]]
+                normed = normed_rows(
+                    rows.reshape(HALF, SHARE[m]), rate[slots], gains[rel, 0:1, KEEP[m] :]
+                )
+                term = dot(normed, w13[columns_of(rel, KEEP[m], SHARE[m]), :])
+                value = term if value is None else value + term
+            acc[slots, :] += value
 
     def activate(m):
         gated, lifted = acc[:, :FF], acc[:, FF:]
@@ -507,7 +516,6 @@
     msg.wait(ahead_come_r[0])
     msg.wait(ahead_come_l[0])
     expert_in(0, OPPOSITE)
-    msg.wait(all_come[0])
     expert_in_all(0)
     activate(0)
     for c in range(CUTS):
@@ -526,7 +534,6 @@
     msg.wait(ahead_come_r[1])
     msg.wait(ahead_come_l[1])
     expert_in(1, OPPOSITE)
-    msg.wait(all_come[1])
     expert_in_all(1)
     activate(1)
     send_opposite(1, 0)

time: 99.8 us -> 100 us (level)
  no operation moved by 1% of the time
where the time goes in v5:
time: 100 us; the launch traced here: 99.9 us
  Pallas kernels  96.2 us (96%)
  local copies, waits for them, and re-layouts  3.04 us (3%)
    pallas_call x1, Pallas kernels, per_device(): pl.pallas_call(kernel, out_shape=(jax.ShapeDtypeStruct((MICRO, ROWS, PART...  96.2 us
    unnamed x2, local copies, waits for them, and re-layouts  3.04 us

profile of v5, /device:TPU:32, one launch (start us, length us, event | category | flops | bytes accessed | tf_op | source)
XLA Modules:
  0.0 99.9 jit_solution(7393429409960619521)
XLA Ops:
  0.6 96.2 %shard_map.122 = (bf16[2,64,1024]{2,1,0:T(8,128)(2,1)}, bf16[2,64,128]{2,1,0:T(8,128)(2,1)}) custom-call(bf16[2,64,1024]{2,1,0:T(8,128)(2,1)} %bitcast.21, s32[2,2,64]{2,1,0:T(2,128)} %bitcast.22, f32[2,2,64]{2,1,0:T(2,128)} %bitcast.23, bf16[1,1024]{1,0:T(2,128)(2,1)} %mgain_hbm.1, bf16[1,1024]{1,0:T(2,128)(2,1)} %again_hbm.1, bf16[4096,384]{1,0:T(8,128)(2,1)} %bitcast.16, ...), custom_call_target="tpu_custom_call" | custom-call | flops 5299999744 | bytes 13000000 | tf_op jit(solution)/shard_map/pallas_call | solution.py:621
  96.8 1.7 %copy.15 = bf16[1,2,64,1024]{3,2,1,0:T(8,128)(2,1)} copy(bf16[1,2,64,1024]{3,2,1,0:T(8,128)(2,1)} %bitcast.14) | data formatting | bytes 524288
  98.5 1.4 %copy.16 = bf16[1,2,64,128]{3,2,1,0:T(8,128)(2,1)} copy(bf16[1,2,64,128]{3,2,1,0:T(8,128)(2,1)} %bitcast.15) | data formatting | bytes 65536
